TPU v7x, 32 devices: a whole 2x2x4 slice. The times are simulated.
32 devices in a mesh: tmpl: 8 (over z, x), sta: 4 (over y, core).
Axes of the slice: x: 2, y: 2, z: 4, core: 2. Of those that a mesh axis runs over, the one named last changes fastest.
Arguments:
- waveforms: bfloat16 [2048, 3, 1664], P(('tmpl', 'sta')), may hold values from -70 to 70, as said below
- templates: bfloat16 [256, 20, 3, 1024], P(('tmpl', 'sta')), may hold values from -0.5 to 1.5
- stations: int32 [256, 20], P(('tmpl', 'sta')), may hold values from 0 to 2047, as said below
- moveouts: int32 [256, 20], P(('tmpl', 'sta')), may hold values from 0 to 384
Outputs:
- stacks: float32 [256, 256], P(('tmpl', 'sta'))
- strongest: float32 [256], replicated
Inputs may be any that keep to these rules, and one draw needn't show every extreme that they name: Station s lies on device s // 64 in the order of tmpl+sta. Of the 160 entries of the templates on one device, at most 10 name stations of one device. `waveforms`: recorded traces of order one to tens.
All inputs are finite; a program needn't handle non-finite values.
Results may differ from a plain program's by a relative error of at most 0.0029.
Values may be sent and summed in bfloat16 or wider, within the bound.
No kernel may reach another device: no remote copies, remote signals or barrier semaphores. Data moves between devices by JAX's collectives and lax.ppermute only.
A program may use at most 64 MiB of HBM per device.

v0:
```python
import functools
import math

import jax
import jax.numpy as jnp
import ml_dtypes
import numpy as np
from jax import lax
from jax.experimental import pallas as pl
from jax.experimental.pallas import tpu as pltpu
from jax.sharding import PartitionSpec as P

LAGS = 256
HALF = "half"
GROUP = ("tmpl", "sta")
AXES = (HALF,) + GROUP
SOURCES = 4
ROWS = 16
DIGITS = 3
LANES = 128
MIB = 1024 * 1024


def bits_of(limit):
    return max(1, (limit - 1).bit_length())


def split_table(table):
    high = table.astype(ml_dtypes.bfloat16)
    return high, (table - high.astype(np.float64)).astype(ml_dtypes.bfloat16)


def transform_table(piece):
    size = 2 * piece
    angle = 2.0 * np.pi * (np.arange(piece) + 0.5) / size
    phase = np.arange(piece)[:, None] * angle[None, :]
    forward = np.concatenate([np.cos(phase), -np.sin(phase)], axis=1)
    inverse = np.concatenate([np.cos(phase.T), -np.sin(phase.T)], axis=0) * (2.0 / size)
    return np.concatenate([*split_table(forward), np.concatenate(split_table(inverse), axis=1)], axis=0)


def edge_table(lag_count):
    sample = np.arange(lag_count)[:, None]
    lag = np.arange(lag_count)[None, :]
    return np.concatenate([sample >= lag, sample < lag], axis=0).astype(ml_dtypes.bfloat16)


def iota(shape, axis):
    return lax.broadcasted_iota(jnp.int32, shape, axis)


def dot(a, b):
    return jnp.dot(a, b, preferred_element_type=jnp.float32)


def exact_dot(a, b):
    return jnp.dot(a, b, precision=lax.Precision.HIGHEST, preferred_element_type=jnp.float32)


def entry_lanes(tpl_count, slot_count):
    pairs = tpl_count * slot_count
    first = iota((slot_count, pairs), 0) * tpl_count
    entry = iota((slot_count, pairs), 1)
    spread = jnp.where((entry >= first) & (entry < first + tpl_count), 1.0, 0.0)
    start = jnp.sum(spread * first.astype(jnp.float32), axis=0, keepdims=True)
    return spread, iota((1, pairs), 1).astype(jnp.float32) - start


def as_lanes(values, spread, place, tpl_count):
    owners = values.shape[0] // tpl_count
    pairs = spread.shape[1]
    wide = exact_dot(values.astype(jnp.float32), spread).reshape(owners, tpl_count, pairs)
    own = iota((1, tpl_count, pairs), 1).astype(jnp.float32) == place.reshape(1, 1, pairs)
    return jnp.sum(jnp.where(own, wide, 0.0), axis=1)


def count_before(hits):
    pairs = hits.shape[1]
    earlier = jnp.where(iota((pairs, pairs), 0) < iota((pairs, pairs), 1), 1.0, 0.0)
    return dot(hits.astype(jnp.bfloat16), earlier.astype(jnp.bfloat16))


def first_kernel(
    cfg, half_ref, stations_ref, moveouts_ref, templates_hbm, first_hbm, shapes_hbm, place_ref, raw_ref, shapes_ref, packed_ref, sems
):
    load = pltpu.make_async_copy(templates_hbm, raw_ref, sems.at[0])
    load.start()
    tpl_count, slot_count = stations_ref.shape
    pairs = tpl_count * slot_count
    devices, group, halves, comps = cfg["devices"], cfg["group"], cfg["halves"], cfg["comps"]
    station_dev, capacity = cfg["station_dev"], cfg["capacity"]
    spread, place = entry_lanes(tpl_count, slot_count)
    station = as_lanes(stations_ref[...], spread, place, tpl_count)
    shift = as_lanes(moveouts_ref[...], spread, place, tpl_count)
    device = jnp.floor((station + 0.5) * (1.0 / station_dev))
    onehot = jnp.where(iota((devices, pairs), 0).astype(jnp.float32) == device, 1.0, 0.0)
    rank = jnp.sum(onehot * count_before(onehot), axis=0, keepdims=True)
    half = jnp.floor((device + 0.5) * (1.0 / group))
    holder = device - half * group
    away = jnp.where(half == half_ref[0].astype(jnp.float32), 0.0, 1.0)
    base = jnp.where(rank < float(capacity), away * (comps * capacity) + rank, -1e6)
    place_ref[0:1, :] = base
    place_ref[1:2, :] = holder

    code = ((place + 1.0) * (1 << cfg["row_bits"]) + station - device * station_dev) * (1 << cfg["shift_bits"]) + shift
    code = code.astype(jnp.int32)
    at_rank = jnp.where(iota((LANES, pairs), 0).astype(jnp.float32) == rank, 1.0, 0.0).astype(jnp.bfloat16)
    at_holder = iota((group, pairs), 0).astype(jnp.float32) == holder
    digits = []
    for q in range(halves):
        for d in range(DIGITS):
            digit = (lax.shift_right_logical(code, 8 * d) & 255).astype(jnp.float32)
            marked = jnp.where(at_holder & (away == float(q)), digit, 0.0).astype(jnp.bfloat16)
            digits.append(
                lax.dot_general(marked, at_rank, (((1,), (1,)), ((), ())), preferred_element_type=jnp.float32)
            )
    codes = jnp.concatenate(digits, axis=1)
    width = codes.shape[1]
    codes = jnp.broadcast_to(codes.reshape(group, 1, width), (group, ROWS, width))
    last = iota((group, ROWS, 1), 1) == ROWS - 1
    codes = jnp.where(last, codes, 0.0).reshape(group * ROWS, width)

    load.wait()
    length = raw_ref.shape[3]
    for c in range(comps):
        values = raw_ref[:, c].astype(jnp.float32).reshape(pairs, length)
        centred = values - jnp.mean(values, axis=-1, keepdims=True)
        spread_c = jnp.sqrt(jnp.mean(centred * centred, axis=-1, keepdims=True) + 1e-05)
        shapes_ref[c] = (centred * (1.0 / spread_c)).astype(jnp.bfloat16)
    keep = pltpu.make_async_copy(shapes_ref, shapes_hbm, sems.at[1])
    keep.start()
    total = pick_rows(cfg, base, holder, 0, ROWS - 1, ROWS, 0, group, shapes_ref)
    total = jnp.concatenate([total[:, :width] + codes, total[:, width:]], axis=1)
    packed_ref[...] = total.astype(jnp.bfloat16)
    send = pltpu.make_async_copy(packed_ref, first_hbm, sems.at[2])
    send.start()
    keep.wait()
    send.wait()


def pick_rows(cfg, base, holder, low, count, rows, start, holders, shapes_ref):
    comps, pairs, length = shapes_ref.shape
    line = iota((holders * rows, pairs), 0).astype(jnp.float32)
    total = jnp.zeros((holders * rows, length), jnp.float32)
    for c in range(comps):
        local = base + float(c * cfg["capacity"] - low)
        inside = (local >= 0.0) & (local < float(count))
        goal = jnp.where(inside, (holder - float(start)) * rows + local, -1.0)
        pick = jnp.where(line == goal, 1.0, 0.0).astype(jnp.bfloat16)
        total = total + dot(pick, shapes_ref[c])
    return total


def rest_kernel(cfg, place_ref, shapes_hbm, rest_hbm, shapes_ref, packed_ref, in_sem, out_sems):
    load = pltpu.make_async_copy(shapes_hbm, shapes_ref, in_sem)
    load.start()
    base, holder = place_ref[0:1, :], place_ref[1:2, :]
    load.wait()
    tile = SOURCES * cfg["rest"]
    copies = []
    for step in range(packed_ref.shape[0] // tile):
        part = pl.ds(step * tile, tile)
        total = pick_rows(
            cfg, base, holder, ROWS - 1, cfg["rest"], cfg["rest"], step * SOURCES, SOURCES, shapes_ref
        )
        packed_ref[part, :] = total.astype(jnp.bfloat16)
        copies.append(pltpu.make_async_copy(packed_ref.at[part], rest_hbm.at[part], out_sems.at[step]))
        copies[-1].start()
    for copy in copies:
        copy.wait()


def read_codes(first_block, block):
    width = DIGITS * LANES
    rows = first_block.shape[0] // SOURCES
    values = first_block[:, block * width : (block + 1) * width].astype(jnp.float32).reshape(SOURCES, rows, width)
    last = iota((1, rows, 1), 1) == rows - 1
    digits = jnp.sum(jnp.where(last, values, 0.0), axis=1)
    return sum(digits[:, d * LANES : (d + 1) * LANES] * float(256**d) for d in range(DIGITS))


def block_lines(cfg, codes, first, rows, count):
    capacity, comps, halves = cfg["capacity"], cfg["comps"], cfg["halves"]
    tile = SOURCES * rows
    row = iota((SOURCES, rows, 1), 1).reshape(tile, 1)
    owner = iota((SOURCES, rows, 1), 0).reshape(tile, 1)
    line = row + first
    panel = jnp.zeros((tile, 1), jnp.int32)
    for m in range(1, halves * comps + 1):
        panel = panel + jnp.where(line >= m * capacity, 1, 0)
    slot = line - panel * capacity
    valid = (row < count) & (panel < halves * comps)
    code = jnp.zeros((tile, 1), jnp.float32)
    for q in range(halves):
        mine = valid & (panel >= q * comps) & (panel < (q + 1) * comps)
        chosen = (iota((tile, LANES), 1) == slot) & mine
        repeated = jnp.broadcast_to(codes[q].reshape(SOURCES, 1, LANES), (SOURCES, rows, LANES)).reshape(tile, LANES)
        code = code + jnp.sum(jnp.where(chosen, repeated, 0.0), axis=1, keepdims=True)
    code = code.astype(jnp.int32)
    shift_bits, row_bits = cfg["shift_bits"], cfg["row_bits"]
    shift = code & ((1 << shift_bits) - 1)
    station = lax.shift_right_logical(code, shift_bits) & ((1 << row_bits) - 1)
    tpl = lax.shift_right_logical(code, shift_bits + row_bits) - 1
    goal = jnp.where(tpl >= 0, panel * cfg["station_dev"] + station, -1)
    return shift, goal, jnp.where(tpl >= 0, owner * cfg["tpl_count"] + tpl, -1)


def cut_traces(cfg, shift, goal, waves):
    tile, seg_len, shift_bits = shift.shape[0], cfg["seg_len"], cfg["shift_bits"]
    pick = jnp.where(iota((tile, waves.shape[0]), 1) == goal, 1.0, 0.0).astype(jnp.bfloat16)
    x = dot(pick, waves).astype(jnp.bfloat16)

    def choose(step, moved, still):
        flag = jnp.where((shift & step) != 0, 1.0, 0.0)
        return moved * flag.astype(jnp.bfloat16) + still * (1.0 - flag).astype(jnp.bfloat16)

    for bit in range(shift_bits - 1, 6, -1):
        step = 1 << bit
        width = seg_len + step
        if x.shape[1] < width + step:
            x = jnp.concatenate([x, jnp.zeros((tile, width + step - x.shape[1]), jnp.bfloat16)], axis=1)
        x = choose(step, x[:, step : step + width], x[:, :width])
    for bit in range(min(shift_bits, 7) - 1, -1, -1):
        step = 1 << bit
        x = choose(step, pltpu.roll(x, x.shape[1] - step, 1), x)
    return x[:, :seg_len]


def line_sums(cfg, column):
    groups = SOURCES * cfg["tpl_count"]
    return jnp.where(iota((column.shape[0], groups), 1) == column, 1.0, 0.0).T.astype(jnp.bfloat16)


def levels_scale(cfg, narrow, edges):
    length = cfg["length"]
    ends = jnp.concatenate([narrow[:, :LAGS], narrow[:, length:]], axis=1).astype(jnp.float32)
    ends = ends * ends
    high = ends.astype(jnp.bfloat16)
    low = (ends - high.astype(jnp.float32)).astype(jnp.bfloat16)
    middle = narrow[:, LAGS:length].astype(jnp.float32)
    energy = dot(high, edges) + dot(low, edges) + jnp.sum(middle * middle, axis=1, keepdims=True)
    return 1.0 / (length * jnp.sqrt(energy * (1.0 / length) + 1e-05))


def shape_spectra(shapes, forward):
    spectra = []
    for h in range(shapes.shape[1] // LAGS):
        part = shapes[:, h * LAGS : (h + 1) * LAGS]
        mine = dot(jnp.concatenate([part, part], axis=1), forward)
        spectra.append((mine[:, :LAGS], mine[:, LAGS:]))
    return spectra


def match_lines(mine, theirs, scale, inverse):
    real = imag = 0.0
    for (mine_r, mine_i), (theirs_r, theirs_i) in zip(mine, theirs):
        real = real + (theirs_r * mine_r + theirs_i * mine_i)
        imag = imag + (theirs_i * mine_r - theirs_r * mine_i)
    product = jnp.concatenate([real, imag], axis=1)
    high = product.astype(jnp.bfloat16)
    low = (product - high.astype(jnp.float32)).astype(jnp.bfloat16)
    return dot(jnp.concatenate([high, high, low], axis=1), inverse) * scale


def sum_lines(sums, left):
    total = 0.0
    for _ in range(3):
        part = left.astype(jnp.bfloat16)
        left = left - part.astype(jnp.float32)
        total = total + dot(sums, part)
    return total


def tables_of(table_ref):
    back = table_ref[2 * LAGS :, :]
    high, low = back[:, :LAGS], back[:, LAGS:]
    return table_ref[: 2 * LAGS, :], jnp.concatenate([high, low, high], axis=0)


def trace_kernel(cfg, first_ref, *refs):
    waves_refs, (table_ref, edges_ref, sent_ref, kept_ref, sums_ref) = refs[:-5], refs[-5:]
    codes = [read_codes(first_ref[...], q) for q in range(cfg["halves"])]
    early = block_lines(cfg, codes, 0, ROWS, ROWS - 1)
    late = block_lines(cfg, codes, ROWS - 1, cfg["rest"], cfg["rest"])
    split = SOURCES * ROWS
    shift, goal = (jnp.concatenate([early[k], late[k]], axis=0) for k in range(2))
    waves = [ref[...].reshape(-1, ref.shape[2]) for ref in waves_refs]
    narrow = cut_traces(cfg, shift, goal, jnp.concatenate(waves, axis=0))
    scale = levels_scale(cfg, narrow, edges_ref[...])
    kept_ref[:, 2 * cfg["length"] :] = scale[split:]
    sums_ref[...] = line_sums(cfg, late[2])

    forward, inverse = tables_of(table_ref)
    sign = (1 - 2 * (iota((1, LAGS), 1) & 1)).astype(jnp.float32)
    before = None
    spectra = []
    for h in range(cfg["length"] // LAGS + 1):
        part = narrow[:, h * LAGS : (h + 1) * LAGS]
        here = dot(jnp.concatenate([part, part], axis=1), forward)
        here = here[:, :LAGS], here[:, LAGS:]
        if before is not None:
            real, imag = before[0] + sign * here[1], before[1] - sign * here[0]
            kept_ref[:, (2 * h - 2) * LAGS : (2 * h - 1) * LAGS] = real[split:]
            kept_ref[:, (2 * h - 1) * LAGS : 2 * h * LAGS] = imag[split:]
            spectra.append((real[:split], imag[:split]))
        before = here
    left = match_lines(shape_spectra(first_ref[...], forward), spectra, scale[:split], inverse)
    sent_ref[...] = sum_lines(line_sums(cfg, early[2]), left)


def match_kernel(tiles, shapes_hbm, kept_hbm, sums_hbm, table_hbm, before_hbm, sent_ref, *scratch):
    shapes_ref, kept_ref, sums_ref, table_ref, before_ref, sems = scratch
    tile = shapes_ref.shape[0] // tiles
    groups = sent_ref.shape[0] // tiles
    length = shapes_ref.shape[1]
    copies = []

    def fetch(source, buffer, part=None):
        if part is not None:
            source, buffer = source.at[part], buffer.at[part]
        copies.append(pltpu.make_async_copy(source, buffer, sems.at[len(copies)]))
        copies[-1].start()
        return copies[-1]

    lines = [pl.ds(t * tile, tile) for t in range(tiles)]
    halves = [pl.ds(q * 2 * LAGS, 2 * LAGS) for q in range(2)]
    forward = fetch(table_hbm, table_ref, halves[0])
    shapes, kept = [], []
    for t in range(tiles):
        shapes.append(fetch(shapes_hbm, shapes_ref, lines[t]))
        kept.append(fetch(kept_hbm, kept_ref, lines[t]))
        if t == 0:
            inverse = fetch(table_hbm, table_ref, halves[1])
            sums = fetch(sums_hbm, sums_ref)
            before = fetch(before_hbm, before_ref)
    forward.wait()
    for t in range(tiles):
        shapes[t].wait()
        mine = shape_spectra(shapes_ref[lines[t], :], table_ref[: 2 * LAGS, :])
        kept[t].wait()
        theirs = kept_ref[lines[t], :]
        spectra = [
            (theirs[:, 2 * h * LAGS : (2 * h + 1) * LAGS], theirs[:, (2 * h + 1) * LAGS : (2 * h + 2) * LAGS])
            for h in range(length // LAGS)
        ]
        if t == 0:
            for copy in (inverse, sums, before):
                copy.wait()
        left = match_lines(mine, spectra, theirs[:, 2 * length :], tables_of(table_ref)[1])
        ends = pl.ds(t * groups, groups)
        sent_ref[ends, :] = before_ref[ends, :] + sum_lines(sums_ref[ends, :], left)


def stack_kernel(factor, parts_ref, stacks_ref, top_ref):
    stacks = jnp.sum(parts_ref[...], axis=0) * factor
    stacks_ref[...] = stacks
    top_ref[...] = jnp.broadcast_to(jnp.max(stacks, axis=0, keepdims=True), top_ref.shape)


def body(waveforms, templates, stations, moveouts):
    devices, group, halves = lax.axis_size(AXES), lax.axis_size(GROUP), lax.axis_size(HALF)
    tpl_count, slot_count = stations.shape
    comps, length = templates.shape[2:]
    station_dev, _, samples = waveforms.shape
    seg_len = length + LAGS
    pairs = tpl_count * slot_count
    capacity = (2 * pairs + devices - 1) // devices
    rest = max(1, -(-(halves * comps * capacity - (ROWS - 1)) // 16)) * 16
    cfg = dict(
        devices=devices,
        group=group,
        halves=halves,
        station_dev=station_dev,
        tpl_count=tpl_count,
        comps=comps,
        capacity=capacity,
        rest=rest,
        length=length,
        seg_len=seg_len,
        shift_bits=bits_of(samples - seg_len + 1),
        row_bits=bits_of(station_dev),
    )
    table = jnp.asarray(transform_table(LAGS))
    edges = jnp.asarray(edge_table(LAGS))
    tiles = group // SOURCES
    tile = SOURCES * rest
    lines = group * rest
    sums_tile = SOURCES * tpl_count
    kept_len = 2 * length + LAGS
    whole = pl.BlockSpec(memory_space=pltpu.VMEM)
    anywhere = pl.BlockSpec(memory_space=pl.ANY)
    params = pltpu.CompilerParams(vmem_limit_bytes=60 * MIB)
    by_slot = templates.transpose(1, 2, 0, 3)
    waves = waveforms.transpose(1, 0, 2)
    half = lax.axis_index(HALF).reshape(1)

    def work(flops, size):
        return pl.CostEstimate(flops=flops, bytes_accessed=size, transcendentals=0)

    def exchange(x, axes):
        return lax.all_to_all(x, axes, split_axis=0, concat_axis=0, tiled=True)

    def same(shape):
        return pl.BlockSpec(shape, lambda i: (0,) * len(shape))

    def tiled(*shape):
        return pl.BlockSpec(shape, lambda i: (i, 0))

    traces = [waves] + [lax.ppermute(waves, HALF, [(0, 1), (1, 0)])] * (halves - 1)
    first, shapes, place = pl.pallas_call(
        functools.partial(first_kernel, cfg),
        out_shape=[
            jax.ShapeDtypeStruct((group * ROWS, length), jnp.bfloat16),
            jax.ShapeDtypeStruct((comps, pairs, length), jnp.bfloat16),
            jax.ShapeDtypeStruct((8, pairs), jnp.float32),
        ],
        in_specs=[pl.BlockSpec(memory_space=pltpu.SMEM), whole, whole, anywhere],
        out_specs=[anywhere, anywhere, whole],
        scratch_shapes=[
            pltpu.VMEM(by_slot.shape, jnp.bfloat16),
            pltpu.VMEM((comps, pairs, length), jnp.bfloat16),
            pltpu.VMEM((group * ROWS, length), jnp.bfloat16),
            pltpu.SemaphoreType.DMA((3,)),
        ],
        compiler_params=params,
        cost_estimate=work(1, 1),
        name="first",
    )(half, stations, moveouts, by_slot)
    later = pl.pallas_call(
        functools.partial(rest_kernel, cfg),
        out_shape=jax.ShapeDtypeStruct((lines, length), jnp.bfloat16),
        in_specs=[whole, anywhere],
        out_specs=anywhere,
        scratch_shapes=[
            pltpu.VMEM((comps, pairs, length), jnp.bfloat16),
            pltpu.VMEM((lines, length), jnp.bfloat16),
            pltpu.SemaphoreType.DMA,
            pltpu.SemaphoreType.DMA((tiles,)),
        ],
        compiler_params=params,
        cost_estimate=work(5 * 10**9, 1),
        name="rest",
    )(place, shapes)
    first = exchange(first.reshape(group, ROWS, length), GROUP).reshape(group * ROWS, length)
    first, later = lax.optimization_barrier((first, later))
    arrived = exchange(later.reshape(group, rest, length), GROUP).reshape(lines, length)

    before, kept, sums = pl.pallas_call(
        functools.partial(trace_kernel, cfg),
        grid=(tiles,),
        out_shape=[
            jax.ShapeDtypeStruct((group * tpl_count, LAGS), jnp.float32),
            jax.ShapeDtypeStruct((lines, kept_len), jnp.float32),
            jax.ShapeDtypeStruct((group * tpl_count, tile), jnp.bfloat16),
        ],
        in_specs=[tiled(SOURCES * ROWS, length)]
        + [same(waves.shape)] * halves
        + [same(table.shape), same(edges.shape)],
        out_specs=[tiled(sums_tile, LAGS), tiled(tile, kept_len), tiled(sums_tile, tile)],
        compiler_params=params,
        cost_estimate=work(10**12, 1),
        name="traces",
    )(first, *traces, table, edges)
    operands = (arrived, kept, sums, table, before)
    sent = pl.pallas_call(
        functools.partial(match_kernel, tiles),
        out_shape=jax.ShapeDtypeStruct((group * tpl_count, LAGS), jnp.float32),
        in_specs=[anywhere] * len(operands),
        out_specs=whole,
        scratch_shapes=[pltpu.VMEM(x.shape, x.dtype) for x in operands]
        + [pltpu.SemaphoreType.DMA((4 + 2 * tiles,))],
        compiler_params=pltpu.CompilerParams(vmem_limit_bytes=57 * MIB),
        name="match",
    )(*operands)

    parts = exchange(sent.reshape(group, tpl_count, LAGS), GROUP)
    stacks, top = pl.pallas_call(
        functools.partial(stack_kernel, math.sqrt(length / (comps * slot_count))),
        out_shape=[
            jax.ShapeDtypeStruct((tpl_count, LAGS), jnp.float32),
            jax.ShapeDtypeStruct((devices, 1, LAGS), jnp.float32),
        ],
        in_specs=[whole],
        out_specs=[whole, whole],
        compiler_params=pltpu.CompilerParams(vmem_limit_bytes=16 * MIB),
        name="stack",
    )(parts)
    return stacks, jnp.max(exchange(top, AXES), axis=(0, 1))


def solution(mesh):
    slow, fast = (mesh.shape[name] for name in GROUP)
    halves = 2 if slow % 2 == 0 else 1
    split = jax.sharding.Mesh(mesh.devices.reshape(halves, slow // halves, fast), AXES)
    placed = (
        P(AXES, None, None),
        P(AXES, None, None, None),
        P(AXES, None),
        P(AXES, None),
    )
    return jax.shard_map(body, mesh=split, in_specs=placed, out_specs=(P(AXES, None), P()), check_vma=False)
```

profile of v0, /device:TPU:0, one launch (start us, length us, event | category | flops | bytes accessed | tf_op | source)
XLA Modules:
  0.0 92.0 jit_solution(14255941296435616074)
XLA Ops:
  0.6 0.0 copy-start.1
  0.6 4.5 %first.1 = (bf16[256,1024]{1,0:T(8,128)(2,1)}, bf16[3,160,1024]{2,1,0:T(8,128)(2,1)}, f32[8,160]{1,0:T(8,128)}) custom-call(s32[1]{0:T(128)} %bitcast.half_ref, s32[8,20]{1,0:T(8,128)} %stations_ref.1, s32[8,20]{1,0:T(8,128)} %moveouts_ref.1, bf16[20,3,8,1024]{3,2,1,0:T(8,128)(2,1)} %bitcast.9), custom_call_target="tpu_custom_call" | custom-call | flops 1 | bytes 1 | tf_op jit(solution)/shard_map/first/pallas_call | solution.py:410
  5.1 6.3 %all-to-all-start = ((bf16[16,16,1024]{2,1,0:T(8,128)(2,1)}), bf16[16,16,1024]{2,1,0:T(8,128)(2,1)S(1)}, u32[]{:S(2)}, u32[]{:S(2)}) async-start(bf16[16,16,1024]{2,1,0:T(8,128)(2,1)} %bitcast.12), calls=%async_computation | async-start | bytes 1048576 | tf_op jit(solution)/shard_map/all_to_all | solution.py:401
  11.4 0.0 copy-done.1
  11.4 2.7 %collective-permute-start = (bf16[3,64,1664]{2,1,0:T(8,128)(2,1)S(1)}, bf16[3,64,1664]{2,1,0:T(8,128)(2,1)S(1)}, u32[]{:S(2)}, u32[]{:S(2)}) collective-permute-start(bf16[3,64,1664]{2,1,0:T(8,128)(2,1)S(1)} %bitcast.14), channel_id=1, source_target_pairs={{0,16},{16,0},{1,17},{17,1},{2,18},{18,2},{3,19},{19,3},{4,20},{20... | collective-permute-start | bytes 1916936 | tf_op jit(solution)/shard_map/ppermute | solution.py:409
  14.1 4.1 %rest.1 = bf16[768,1024]{1,0:T(8,128)(2,1)} custom-call(f32[8,160]{1,0:T(8,128)} %get-tuple-element.13.place_ref, bf16[3,160,1024]{2,1,0:T(8,128)(2,1)} %get-tuple-element.14.shapes_hbm), custom_call_target="tpu_custom_call" | custom-call | flops 5000000000 | bytes 1 | tf_op jit(solution)/shard_map/rest/pallas_call | solution.py:429
  18.2 10.4 %all-to-all-done = bf16[16,16,1024]{2,1,0:T(8,128)(2,1)S(1)} async-done(((bf16[16,16,1024]{2,1,0:T(8,128)(2,1)}), bf16[16,16,1024]{2,1,0:T(8,128)(2,1)S(1)}, u32[]{:S(2)}, u32[]{:S(2)}) %all-to-all-start) | async-done | bytes 524320 | tf_op jit(solution)/shard_map/all_to_all | solution.py:401
  28.6 0.0 copy-start
  28.6 0.8 copy-done
  29.4 4.4 %all-to-all-start.1 = ((bf16[16,48,1024]{2,1,0:T(8,128)(2,1)}), bf16[16,48,1024]{2,1,0:T(8,128)(2,1)}, u32[]{:S(2)}, u32[]{:S(2)}) async-start(bf16[16,48,1024]{2,1,0:T(8,128)(2,1)} %bitcast.8), calls=%async_computation.1 | async-start | bytes 3145728 | tf_op jit(solution)/shard_map/all_to_all | solution.py:401
  33.8 9.1 %collective-permute-done.refs_1_ = bf16[3,64,1664]{2,1,0:T(8,128)(2,1)S(1)} collective-permute-done((bf16[3,64,1664]{2,1,0:T(8,128)(2,1)S(1)}, bf16[3,64,1664]{2,1,0:T(8,128)(2,1)S(1)}, u32[]{:S(2)}, u32[]{:S(2)}) %collective-permute-start) | collective-permute-done | bytes 639008 | tf_op jit(solution)/shard_map/ppermute | solution.py:409
  43.0 0.0 copy-start.2
  43.0 0.9 copy-done.2
  43.8 17.9 %traces.1 = (f32[128,256]{1,0:T(8,128)}, f32[768,2304]{1,0:T(8,128)}, bf16[128,192]{1,0:T(8,128)(2,1)}) custom-call(bf16[256,1024]{1,0:T(8,128)(2,1)} %bitcast.11, bf16[3,64,1664]{2,1,0:T(8,128)(2,1)} %bitcast.13, bf16[3,64,1664]{2,1,0:T(8,128)(2,1)} %copy-done.2, bf16[1024,512]{1,0:T(8,128)(2,1)} %constant.12.clone.refs_2_.table_hbm, ...), custom_call_target="tpu_custom_call" | custom-call | flops 999999995904 | bytes 1 | tf_op jit(solution)/shard_map/traces/pallas_call | solution.py:448
  61.7 0.1 all-to-all-done.1
  61.8 7.8 %match.1 = f32[128,256]{1,0:T(8,128)} custom-call(bf16[768,1024]{1,0:T(8,128)(2,1)} %bitcast.5.shapes_hbm, f32[768,2304]{1,0:T(8,128)} %get-tuple-element.17.kept_hbm, bf16[128,192]{1,0:T(8,128)(2,1)} %get-tuple-element.18.sums_hbm, bf16[1024,512]{1,0:T(8,128)(2,1)} %constant.12.clone.refs_2_.table_hbm, f32[128,256]{1,0:T(8,128)} %get-tuple-element.19.before_hbm), custom_call_target="tpu_custom_call" | custom-call | tf_op jit(solution)/shard_map/match/pallas_call | solution.py:465
  69.7 10.2 %all_to_all.20.parts_ref = f32[16,8,256]{2,1,0:T(8,128)S(1)} all-to-all(f32[16,8,256]{2,1,0:T(8,128)} %bitcast.10), channel_id=1, replica_groups=mesh['half'=2,'tmpl'=4,'sta'=4] {'tmpl','sta'}, dimensions={0} | all-to-all | bytes 262144 | tf_op jit(solution)/shard_map/all_to_all | solution.py:401
  79.9 0.6 stack.1
  80.5 10.9 %all_to_all.21 = f32[32,1,256]{2,1,0:T(1,128)S(1)} all-to-all(f32[32,1,256]{2,1,0:T(1,128)S(1)} %get-tuple-element.21), channel_id=1, replica_groups=mesh['half'=2,'tmpl'=4,'sta'=4] {'half','tmpl','sta'}, dimensions={0} | all-to-all | bytes 65536 | tf_op jit(solution)/shard_map/all_to_all | solution.py:401
  91.4 0.6 reduce_max.9
Async XLA Ops:
  0.6 10.8 %copy-start.1 = (bf16[64,3,1664]{2,0,1:T(8,128)(2,1)S(1)}, bf16[64,3,1664]{2,0,1:T(8,128)(2,1)}, u32[]{:S(2)}) copy-start(bf16[64,3,1664]{2,0,1:T(8,128)(2,1)} %param.6) | copy-start | bytes 1916932
  5.1 23.5 %all-to-all-start = ((bf16[16,16,1024]{2,1,0:T(8,128)(2,1)}), bf16[16,16,1024]{2,1,0:T(8,128)(2,1)S(1)}, u32[]{:S(2)}, u32[]{:S(2)}) async-start(bf16[16,16,1024]{2,1,0:T(8,128)(2,1)} %bitcast.12), calls=%async_computation | async-start | bytes 1048576 | tf_op jit(solution)/shard_map/all_to_all | solution.py:401
  11.4 31.5 %collective-permute-start = (bf16[3,64,1664]{2,1,0:T(8,128)(2,1)S(1)}, bf16[3,64,1664]{2,1,0:T(8,128)(2,1)S(1)}, u32[]{:S(2)}, u32[]{:S(2)}) collective-permute-start(bf16[3,64,1664]{2,1,0:T(8,128)(2,1)S(1)} %bitcast.14), channel_id=1, source_target_pairs={{0,16},{16,0},{1,17},{17,1},{2,18},{18,2},{3,19},{19,3},{4,20},{20... | collective-permute-start | bytes 1916936 | tf_op jit(solution)/shard_map/ppermute | solution.py:409
  28.6 0.8 copy-start
  29.4 32.4 %all-to-all-start.1 = ((bf16[16,48,1024]{2,1,0:T(8,128)(2,1)}), bf16[16,48,1024]{2,1,0:T(8,128)(2,1)}, u32[]{:S(2)}, u32[]{:S(2)}) async-start(bf16[16,48,1024]{2,1,0:T(8,128)(2,1)} %bitcast.8), calls=%async_computation.1 | async-start | bytes 3145728 | tf_op jit(solution)/shard_map/all_to_all | solution.py:401
  43.0 0.9 copy-start.2
where the time goes:
time: 92.5 us; the launch traced here: 92 us
  Pallas kernels  34.9 us (38%)
  blocking collectives  21.1 us (23%)
  waiting for transfers between devices  19.7 us (21%)
  starting transfers between devices  13.4 us (14%)
  local copies, waits for them, and re-layouts  1.69 us (2%)
    all_to_all x2, blocking collectives, exchange(): return lax.all_to_all(x, axes, split_axis=0, concat_axis=0, tiled=True)  21.1 us
    pallas_call x1, Pallas kernels, body(): pl.pallas_call(functools.partial(trace_kernel, cfg), grid=(tiles,), out_s...  17.9 us
    all_to_all x2, starting transfers between devices, exchange(): return lax.all_to_all(x, axes, split_axis=0, concat_axis=0, tiled=True)  10.7 us
    all_to_all x2, waiting for transfers between devices, exchange(): return lax.all_to_all(x, axes, split_axis=0, concat_axis=0, tiled=True)  10.5 us
    ppermute x1, waiting for transfers between devices, body(): lax.ppermute(waves, HALF, [(0, 1), (1, 0)])  9.12 us
    pallas_call x1, Pallas kernels, body(): pl.pallas_call(functools.partial(match_kernel, tiles), out_shape=jax.Shap...  7.85 us
    pallas_call x1, Pallas kernels, body(): pl.pallas_call(functools.partial(first_kernel, cfg), out_shape=[jax.Shape...  4.47 us
    pallas_call x1, Pallas kernels, body(): pl.pallas_call(functools.partial(rest_kernel, cfg), out_shape=jax.ShapeDt...  4.11 us
  transfers between devices with their start and end apart: 3, of which 3 were waited for; matrix products, arithmetic and copies ran while one was open for 0% of the time, Pallas kernels for 24%

commit v1 on v0

--- a/solution.py
+++ b/solution.py
@@ -438,7 +438,7 @@
             pltpu.SemaphoreType.DMA((tiles,)),
         ],
         compiler_params=params,
-        cost_estimate=work(5 * 10**9, 1),
+        cost_estimate=work(10**12, 1),
         name="rest",
     )(place, shapes)
     first = exchange(first.reshape(group, ROWS, length), GROUP).reshape(group * ROWS, length)

time: 92.5 us -> 93.1 us (level)
  waiting for transfers between devices: 19.7 us -> 24.2 us
  blocking collectives: 21.1 us -> 18.7 us
  local copies, waits for them, and re-layouts: 1.69 us -> 0 us
    all_to_all x2, waiting for transfers between devices: 10.5 us -> 24.2 us  [exchange(): return lax.all_to_all(x, axes, split_axis=0, concat_axis=0, tiled=True)]
    ppermute x1, waiting for transfers between devices: 9.12 us -> 0.01 us  [body(): lax.ppermute(waves, HALF, [(0, 1), (1, 0)])]
    all_to_all x2, blocking collectives: 21.1 us -> 18.7 us  [exchange(): return lax.all_to_all(x, axes, split_axis=0, concat_axis=0, tiled=True)]
    unnamed x6 -> x0, local copies, waits for them, and re-layouts: 1.69 us -> none
    ppermute x1, starting transfers between devices: 2.66 us -> 4.1 us  [body(): lax.ppermute(waves, HALF, [(0, 1), (1, 0)])]
    all_to_all x2, starting transfers between devices: 10.7 us -> 9.31 us  [exchange(): return lax.all_to_all(x, axes, split_axis=0, concat_axis=0, tiled=True)]
  transfers between devices with their start and end apart: 3 -> 3, of which waited for: 3 -> 2; matrix products, arithmetic and copies ran while one was open for 0% -> 0% of each run, Pallas kernels for 24% -> 29%
where the time goes in v1:
time: 93.1 us; the launch traced here: 92.5 us
  Pallas kernels  34.9 us (37%)
  waiting for transfers between devices  24.2 us (26%)
  blocking collectives  18.7 us (20%)
  starting transfers between devices  13.4 us (14%)
    all_to_all x2, waiting for transfers between devices, exchange(): return lax.all_to_all(x, axes, split_axis=0, concat_axis=0, tiled=True)  24.2 us
    all_to_all x2, blocking collectives, exchange(): return lax.all_to_all(x, axes, split_axis=0, concat_axis=0, tiled=True)  18.7 us
    pallas_call x1, Pallas kernels, body(): pl.pallas_call(functools.partial(trace_kernel, cfg), grid=(tiles,), out_s...  17.9 us
    all_to_all x2, starting transfers between devices, exchange(): return lax.all_to_all(x, axes, split_axis=0, concat_axis=0, tiled=True)  9.31 us
    pallas_call x1, Pallas kernels, body(): pl.pallas_call(functools.partial(match_kernel, tiles), out_shape=jax.Shap...  7.85 us
    pallas_call x1, Pallas kernels, body(): pl.pallas_call(functools.partial(first_kernel, cfg), out_shape=[jax.Shape...  4.41 us
    pallas_call x1, Pallas kernels, body(): pl.pallas_call(functools.partial(rest_kernel, cfg), out_shape=jax.ShapeDt...  4.11 us
    ppermute x1, starting transfers between devices, body(): lax.ppermute(waves, HALF, [(0, 1), (1, 0)])  4.1 us
  transfers between devices with their start and end apart: 3, of which 2 were waited for; matrix products, arithmetic and copies ran while one was open for 0% of the time, Pallas kernels for 29%

profile of v1, /device:TPU:0, one launch (start us, length us, event | category | flops | bytes accessed | tf_op | source)
XLA Modules:
  0.0 92.5 jit_solution(13409589225827535530)
XLA Ops:
  0.6 4.1 %collective-permute-start = (bf16[3,64,1664]{2,1,0:T(8,128)(2,1)}, bf16[3,64,1664]{2,1,0:T(8,128)(2,1)}, u32[]{:S(2)}, u32[]{:S(2)}) collective-permute-start(bf16[3,64,1664]{2,1,0:T(8,128)(2,1)} %bitcast.12), channel_id=1, source_target_pairs={{0,16},{16,0},{1,17},{17,1},{2,18},{18,2},{3,19},{19,3},{4,20},{20... | collective-permute-start | bytes 1916936 | tf_op jit(solution)/shard_map/ppermute | solution.py:409
  4.7 4.4 %first.1 = (bf16[256,1024]{1,0:T(8,128)(2,1)}, bf16[3,160,1024]{2,1,0:T(8,128)(2,1)}, f32[8,160]{1,0:T(8,128)}) custom-call(s32[1]{0:T(128)} %bitcast.half_ref, s32[8,20]{1,0:T(8,128)} %stations_ref.1, s32[8,20]{1,0:T(8,128)} %moveouts_ref.1, bf16[20,3,8,1024]{3,2,1,0:T(8,128)(2,1)} %bitcast.9), custom_call_target="tpu_custom_call" | custom-call | flops 1 | bytes 1 | tf_op jit(solution)/shard_map/first/pallas_call | solution.py:410
  9.2 4.9 %all-to-all-start = ((bf16[16,16,1024]{2,1,0:T(8,128)(2,1)}), bf16[16,16,1024]{2,1,0:T(8,128)(2,1)}, u32[]{:S(2)}, u32[]{:S(2)}) async-start(bf16[16,16,1024]{2,1,0:T(8,128)(2,1)} %bitcast.11), calls=%async_computation | async-start | bytes 1048576 | tf_op jit(solution)/shard_map/all_to_all | solution.py:401
  14.1 4.1 %rest.1 = bf16[768,1024]{1,0:T(8,128)(2,1)} custom-call(f32[8,160]{1,0:T(8,128)} %get-tuple-element.13.place_ref, bf16[3,160,1024]{2,1,0:T(8,128)(2,1)} %get-tuple-element.14.shapes_hbm), custom_call_target="tpu_custom_call" | custom-call | flops 999999995904 | bytes 1 | tf_op jit(solution)/shard_map/rest/pallas_call | solution.py:429
  18.2 19.1 %all-to-all-done = bf16[16,16,1024]{2,1,0:T(8,128)(2,1)} async-done(((bf16[16,16,1024]{2,1,0:T(8,128)(2,1)}), bf16[16,16,1024]{2,1,0:T(8,128)(2,1)}, u32[]{:S(2)}, u32[]{:S(2)}) %all-to-all-start) | async-done | bytes 524320 | tf_op jit(solution)/shard_map/all_to_all | solution.py:401
  37.2 4.4 %all-to-all-start.1 = ((bf16[16,48,1024]{2,1,0:T(8,128)(2,1)}), bf16[16,48,1024]{2,1,0:T(8,128)(2,1)}, u32[]{:S(2)}, u32[]{:S(2)}) async-start(bf16[16,48,1024]{2,1,0:T(8,128)(2,1)} %bitcast.8), calls=%async_computation.1 | async-start | bytes 3145728 | tf_op jit(solution)/shard_map/all_to_all | solution.py:401
  41.7 0.0 collective-permute-done.refs_1_
  41.7 17.9 %traces.1 = (f32[128,256]{1,0:T(8,128)}, f32[768,2304]{1,0:T(8,128)}, bf16[128,192]{1,0:T(8,128)(2,1)}) custom-call(bf16[256,1024]{1,0:T(8,128)(2,1)} %bitcast.3.first_ref, bf16[3,64,1664]{2,1,0:T(8,128)(2,1)} %bitcast.13, bf16[3,64,1664]{2,1,0:T(8,128)(2,1)} %collective-permute-done.refs_1_, bf16[1024,512]{1,0:T(8,128)(2,1)} %constant.12.clone.refs_2_.table_hbm, ...), custom_call_target="tpu_custom_call" | custom-call | flops 999999995904 | bytes 1 | tf_op jit(solution)/shard_map/traces/pallas_call | solution.py:448
  59.6 5.2 %all-to-all-done.1 = bf16[16,48,1024]{2,1,0:T(8,128)(2,1)} async-done(((bf16[16,48,1024]{2,1,0:T(8,128)(2,1)}), bf16[16,48,1024]{2,1,0:T(8,128)(2,1)}, u32[]{:S(2)}, u32[]{:S(2)}) %all-to-all-start.1) | async-done | bytes 1572896 | tf_op jit(solution)/shard_map/all_to_all | solution.py:401
  64.7 7.8 %match.1 = f32[128,256]{1,0:T(8,128)} custom-call(bf16[768,1024]{1,0:T(8,128)(2,1)} %bitcast.5.shapes_hbm, f32[768,2304]{1,0:T(8,128)} %get-tuple-element.17.kept_hbm, bf16[128,192]{1,0:T(8,128)(2,1)} %get-tuple-element.18.sums_hbm, bf16[1024,512]{1,0:T(8,128)(2,1)} %constant.12.clone.refs_2_.table_hbm, f32[128,256]{1,0:T(8,128)} %get-tuple-element.19.before_hbm), custom_call_target="tpu_custom_call" | custom-call | tf_op jit(solution)/shard_map/match/pallas_call | solution.py:465
  72.6 9.8 %all_to_all.20.parts_ref = f32[16,8,256]{2,1,0:T(8,128)S(1)} all-to-all(f32[16,8,256]{2,1,0:T(8,128)} %bitcast.10), channel_id=1, replica_groups=mesh['half'=2,'tmpl'=4,'sta'=4] {'tmpl','sta'}, dimensions={0} | all-to-all | bytes 262144 | tf_op jit(solution)/shard_map/all_to_all | solution.py:401
  82.4 0.6 stack.1
  83.0 8.9 %all_to_all.21 = f32[32,1,256]{2,1,0:T(1,128)S(1)} all-to-all(f32[32,1,256]{2,1,0:T(1,128)S(1)} %get-tuple-element.21), channel_id=1, replica_groups=mesh['half'=2,'tmpl'=4,'sta'=4] {'half','tmpl','sta'}, dimensions={0} | all-to-all | bytes 65536 | tf_op jit(solution)/shard_map/all_to_all | solution.py:401
  91.9 0.6 reduce_max.9
Async XLA Ops:
  0.6 41.0 %collective-permute-start = (bf16[3,64,1664]{2,1,0:T(8,128)(2,1)}, bf16[3,64,1664]{2,1,0:T(8,128)(2,1)}, u32[]{:S(2)}, u32[]{:S(2)}) collective-permute-start(bf16[3,64,1664]{2,1,0:T(8,128)(2,1)} %bitcast.12), channel_id=1, source_target_pairs={{0,16},{16,0},{1,17},{17,1},{2,18},{18,2},{3,19},{19,3},{4,20},{20... | collective-permute-start | bytes 1916936 | tf_op jit(solution)/shard_map/ppermute | solution.py:409
  9.2 28.1 %all-to-all-start = ((bf16[16,16,1024]{2,1,0:T(8,128)(2,1)}), bf16[16,16,1024]{2,1,0:T(8,128)(2,1)}, u32[]{:S(2)}, u32[]{:S(2)}) async-start(bf16[16,16,1024]{2,1,0:T(8,128)(2,1)} %bitcast.11), calls=%async_computation | async-start | bytes 1048576 | tf_op jit(solution)/shard_map/all_to_all | solution.py:401
  37.2 27.5 %all-to-all-start.1 = ((bf16[16,48,1024]{2,1,0:T(8,128)(2,1)}), bf16[16,48,1024]{2,1,0:T(8,128)(2,1)}, u32[]{:S(2)}, u32[]{:S(2)}) async-start(bf16[16,48,1024]{2,1,0:T(8,128)(2,1)} %bitcast.8), calls=%async_computation.1 | async-start | bytes 3145728 | tf_op jit(solution)/shard_map/all_to_all | solution.py:401
